TPU v7x, 32 devices: a whole 2x2x4 slice. The times are simulated.
32 devices in a mesh: area: 4 (over z), dev: 8 (over y, x, core).
Axes of the slice: x: 2, y: 2, z: 4, core: 2. Of those that a mesh axis runs over, the one named last changes fastest.
Arguments:
- wave_fwd: float32 [3, 16384, 128], P(None, ('area', 'dev')), may hold values from -6 to 6
- wave_bwd: float32 [3, 16384, 128], P(None, ('area', 'dev')), may hold values from -6 to 6
- seg_reflect: float32 [3, 16384], P(None, ('area', 'dev')), may hold values from 0.04 to 0.4
- seg_count: int32 [32, 64], P(('area', 'dev')), may hold values from 1 to 24, 512 in all within a row
- modal_admit: float32 [3, 2048], P(None, ('area', 'dev')), may hold values from 0.02 to 0.2
- modal_transform: float32 [3, 3], replicated, may hold values from -3.5 to 3.5
- end_slot: int32 [2048, 2], P(('area', 'dev')), may hold values from 0 to 255, as said below
- recv_bus: int32 [32, 256], P(('area', 'dev')), may hold values from -1 to 63, as said below
- bus_impedance: float32 [3, 3, 2048], P(None, None, ('area', 'dev')), as said below
- link_bus: int32 [192, 2], P('area'), may hold values from 0 to 511, as said below
- link_resist: float32 [192], P('area'), may hold values from 0.5 to 5
- source_current: float32 [4, 2048, 3, 128], P(None, ('area', 'dev')), may hold values from -6 to 6
Outputs:
- bus_voltage: float32 [4, 2048, 3, 128], P(None, ('area', 'dev'))
- final_fwd: float32 [3, 16384, 128], P(None, ('area', 'dev'))
- final_bwd: float32 [3, 16384, 128], P(None, ('area', 'dev'))
Inputs may be any that keep to these rules, and one draw needn't show every extreme that they name: `end_slot`: entry [l, s] is the slot of end s (0 sending, 1 receiving) of line l within its device's 32 blocks of 8 slots, block q // 8 going to owner device q // 8. The slots of one device are distinct. Every device fills all 8 slots of the block for some owner, and one owner receives 8 ends from every device. `recv_bus`: row r, column s * 8 + c: the local bus of device r to which slot c of device s's block for r attaches, and -1 exactly where no end of device s holds that slot. `link_bus`: the two buses of a link differ. `bus_impedance`: each bus's 3x3 matrix is symmetric with a positive diagonal larger than the sum of its row's other magnitudes.
All inputs are finite; a program needn't handle non-finite values.
Results may differ from a plain program's by a relative error of at most 0.00012.
Values sent between devices are 32-bit elements; how exact they have to be, the bound alone decides.
A program may use at most 64 MiB of HBM per device.

v0:
```python
import jax
import jax.numpy as jnp
from jax import lax
from jax.sharding import PartitionSpec as P

STEPS = 4


def solve_links(factor, rhs):
    lower = lax.linalg.triangular_solve(factor, rhs, left_side=True, lower=True)
    return lax.linalg.triangular_solve(factor, lower, left_side=True, lower=True, transpose_a=True)


def send_ends(rows):
    return lax.all_to_all(rows, ("area", "dev"), split_axis=0, concat_axis=0, tiled=True)


def return_volts(rows):
    return lax.all_to_all(rows, ("area", "dev"), split_axis=0, concat_axis=0, tiled=True)


def on_device(
    wave_fwd,
    wave_bwd,
    seg_reflect,
    seg_count,
    modal_admit,
    modal_transform,
    end_slot,
    recv_bus,
    bus_impedance,
    link_bus,
    link_resist,
    source_current,
):
    exact = lax.Precision.HIGHEST
    cases = wave_fwd.shape[2]
    line_total = end_slot.shape[0]
    counts = seg_count[0]
    first = jnp.cumsum(counts) - counts
    last = first + counts - 1
    bus_total = bus_impedance.shape[2]
    link_total = link_bus.shape[0]
    bus_index = jnp.arange(bus_total, dtype=jnp.int32) + lax.axis_index("dev") * bus_total
    incidence = (bus_index[:, None] == link_bus[None, :, 0]).astype(jnp.float32) - (
        bus_index[:, None] == link_bus[None, :, 1]
    ).astype(jnp.float32)
    partial_value = jnp.einsum(
        "bl,ijb,bm->limj", incidence, bus_impedance, incidence, precision=exact
    ).reshape(3 * link_total, 3 * link_total)
    matrix = lax.psum(partial_value, "dev") + jnp.diag(jnp.repeat(link_resist, 3))
    factor = jnp.linalg.cholesky(matrix)
    place_overall_sum = recv_bus.shape[1]
    one_hot = (jnp.arange(bus_total, dtype=jnp.int32)[:, None] == recv_bus).astype(jnp.float32)
    flat_slot = end_slot.reshape(-1)
    reflect_next = jnp.roll(seg_reflect, -1, axis=1)
    forward, backward = (wave_fwd, wave_bwd)
    voltages = []
    for step in range(STEPS):
        arriving = jnp.stack([backward[:, first, :], forward[:, last, :]], axis=2)
        history = 2.0 * jnp.einsum(
            "mi,mlsk->lsik",
            modal_transform,
            modal_admit[:, :, None, None] * arriving,
            precision=exact,
        )
        send_rows = (
            jnp.zeros((place_overall_sum, 3 * cases), jnp.float32)
            .at[flat_slot]
            .set(history.reshape(2 * line_total, 3 * cases))
        )
        received = send_ends(send_rows)
        summed = jnp.dot(
            one_hot, received, precision=exact, preferred_element_type=jnp.float32
        ).reshape(bus_total, 3, cases)
        inject = source_current[step] + summed
        open_volts = jnp.einsum("ijb,bjk->bik", bus_impedance, inject, precision=exact)
        sources = jnp.einsum("bl,bik->lik", incidence, open_volts, precision=exact).reshape(
            3 * link_total, cases
        )
        owned = lax.psum_scatter(sources, "dev", scatter_dimension=1, tiled=True)
        current = lax.all_gather(solve_links(factor, owned), "dev", axis=1, tiled=True)
        current = current.reshape(link_total, 3, cases)
        net = inject - jnp.einsum("bl,lik->bik", incidence, current, precision=exact)
        volts = jnp.einsum("ijb,bjk->bik", bus_impedance, net, precision=exact)
        voltages.append(volts)
        slot_volts = jnp.dot(
            one_hot.T,
            volts.reshape(bus_total, 3 * cases),
            precision=exact,
            preferred_element_type=jnp.float32,
        )
        back_rows = return_volts(slot_volts)
        end_volts = back_rows[flat_slot].reshape(line_total, 2, 3, cases)
        outgoing = (
            jnp.einsum("mi,lsik->mlsk", modal_transform, end_volts, precision=exact) - arriving
        )
        fwd_next = (1.0 - seg_reflect)[:, :, None] * jnp.roll(forward, 1, axis=1) + seg_reflect[
            :, :, None
        ] * backward
        fwd_next = fwd_next.at[:, first, :].set(outgoing[:, :, 0, :])
        bwd_next = (1.0 - reflect_next)[:, :, None] * jnp.roll(backward, -1, axis=1) + reflect_next[
            :, :, None
        ] * forward
        bwd_next = bwd_next.at[:, last, :].set(outgoing[:, :, 1, :])
        forward, backward = (fwd_next, bwd_next)
    return (jnp.stack(voltages), forward, backward)


def solution(mesh):
    in_specs = (
        P(None, ("area", "dev"), None),
        P(None, ("area", "dev"), None),
        P(None, ("area", "dev")),
        P(("area", "dev"), None),
        P(None, ("area", "dev")),
        P(),
        P(("area", "dev"), None),
        P(("area", "dev"), None),
        P(None, None, ("area", "dev")),
        P("area", None),
        P("area"),
        P(None, ("area", "dev"), None, None),
    )
    out_specs = (
        P(None, ("area", "dev"), None, None),
        P(None, ("area", "dev"), None),
        P(None, ("area", "dev"), None),
    )
    return jax.shard_map(
        on_device, mesh=mesh, in_specs=in_specs, out_specs=out_specs, check_vma=False
    )
```

profile of v0, /device:TPU:0, one launch (start us, length us, event | category | flops | bytes accessed | tf_op | source)
XLA Modules:
  0.0 491.2 jit_solution(10305870664416190752)
XLA Ops:
  9.7 1.6 gather_fusion.1
  11.5 1.6 gather_fusion
  14.7 1.7 scatter_custom_fusion
  16.4 7.4 %all-to-all-start = ((f32[32,8,384]{2,1,0:T(8,128)}), f32[32,8,384]{2,1,0:T(8,128)}, u32[]{:S(2)}, u32[]{:S(2)}) async-start(f32[32,8,384]{2,1,0:T(8,128)} %bitcast.11), calls=%async_computation | async-start | bytes 786432 | tf_op jit(solution)/shard_map/all_to_all | solution.py:15
  25.5 2.2 copy.99
  27.7 2.1 reshape.300
  31.9 51.1 %all-reduce.7.cloned.1.call-done = f32[144,144]{1,0:T(8,128)} async-done(((f32[144,144]{1,0:T(8,128)}), f32[144,144]{1,0:T(8,128)}) %all-reduce.7.cloned.1.call-update) | async-done | bytes 82960 | tf_op jit(solution)/shard_map/psum | solution.py:51
  85.2 11.7 %cholesky.50 = f32[128,128]{1,0:T(8,128)S(1)} custom-call(f32[128,128]{1,0:T(8,128)S(1)} %cholesky.121), custom_call_target="Cholesky" | custom-call | tf_op jit(solution)/shard_map/jit(cholesky)/cholesky | solution.py:52
  97.0 9.8 %custom-call.17 = f32[1,128,128]{1,2,0:T(8,128)S(1)} custom-call(f32[1,128,128]{2,1,0:T(8,128)S(1)} %get-tuple-element.103), custom_call_target="InvertDiagBlocksLowerTriangular" | custom-call | tf_op jit(solution)/shard_map/jit(cholesky)/cholesky | solution.py:52
  107.1 1.5 cholesky.108
  111.3 1.2 copy.98
  112.5 1.2 convolution_add_fusion.3
  115.5 19.7 %custom-call.25 = f32[2,128,128]{1,2,0:T(8,128)S(1)} custom-call(f32[2,128,128]{2,1,0:T(8,128)S(1)} %pad_maximum_fusion.9), custom_call_target="InvertDiagBlocksLowerTriangular" | custom-call | tf_op jit(solution)/shard_map/triangular_solve/custom-call.4 | solution.py:11
  135.2 14.8 %reduce-scatter.13.cloned.1.call-done = f32[16,144]{1,0:T(8,128)} async-done(((f32[128,144]{1,0:T(8,128)}), f32[16,144]{1,0:T(8,128)}) %reduce-scatter.13.cloned.1.call-update) | async-done | bytes 9232
  152.5 9.4 %all_gather.12 = f32[144,128]{0,1:T(8,128)S(1)} all-gather(f32[144,16]{0,1:T(8,128)S(1)} %pad_maximum_fusion.10), channel_id=1, replica_groups=mesh['area'=4,'dev'=8] {'dev'}, dimensions={1}, use_global_device_ids=true | all-gather | bytes 82944 | tf_op jit(solution)/shard_map/all_gather | solution.py:82
  164.2 4.6 all-to-all-start.1
  169.1 1.5 copy.234
  170.9 1.5 copy.237
  172.7 5.0 %fusion.5 = f32[3,512,128]{2,0,1:T(4,128)S(1)} fusion(f32[3,511,128]{2,0,1:T(4,128)} %copy.234, f32[3,1,128]{2,0,1:T(4,128)S(1)} %copy.235, f32[3,512]{0,1:T(8,128)S(1)} %copy.117, f32[3,512]{0,1:T(8,128)S(1)} %copy.114, f32[3,512,128]{2,1,0:T(8,128)S(1)} %copy-done.1), kind=kLoop, calls=%fused_computation.61 | loop fusion | flops 786432 | bytes 2371584 | tf_op jit(solution)/shard_map/add | solution.py:98
  177.7 4.5 fusion.4
  183.2 1.6 fusion
  184.8 2.6 scatter_fusion.1
  188.2 2.6 scatter_fusion
  191.5 1.4 convolution_multiply_fusion.2
  193.0 1.2 scatter_custom_fusion.3
  194.3 18.9 %all_to_all.84 = f32[32,8,384]{2,1,0:T(8,128)} all-to-all(f32[32,8,384]{2,1,0:T(8,128)S(1)} %bitcast.344), channel_id=1, replica_groups=mesh['area'=4,'dev'=8] {'area','dev'}, dimensions={0} | all-to-all | bytes 786432 | tf_op jit(solution)/shard_map/all_to_all | solution.py:15
  213.2 1.2 copy.120
  214.4 1.2 convolution_add_fusion.2
  218.0 31.6 %reduce-scatter.15.cloned.1.call-done = f32[16,144]{1,0:T(8,128)} async-done(((f32[128,144]{1,0:T(8,128)}), f32[16,144]{1,0:T(8,128)}) %reduce-scatter.15.cloned.1.call-update) | async-done | bytes 9232
  253.5 9.6 %all_gather.13 = f32[144,128]{0,1:T(8,128)S(1)} all-gather(f32[144,16]{0,1:T(8,128)S(1)} %pad_maximum_fusion.11), channel_id=1, replica_groups=mesh['area'=4,'dev'=8] {'dev'}, dimensions={1}, use_global_device_ids=true | all-gather | bytes 82944 | tf_op jit(solution)/shard_map/all_gather | solution.py:82
  266.0 4.7 all-to-all-start.3
  271.2 3.2 fusion.7
  274.5 2.3 fusion.6
  276.8 7.1 %all-to-all-done.3 = f32[32,8,384]{2,1,0:T(8,128)} async-done(((f32[32,8,384]{2,1,0:T(8,128)}), f32[32,8,384]{2,1,0:T(8,128)}, u32[]{:S(2)}, u32[]{:S(2)}) %all-to-all-start.3) | async-done | bytes 393248 | tf_op jit(solution)/shard_map/all_to_all | solution.py:19
  283.9 2.0 gather_fusion.5
  286.0 1.6 fusion.1
  287.6 2.4 scatter_fusion.3
  290.9 2.4 scatter_fusion.2
  294.8 1.2 scatter_custom_fusion.6
  296.0 15.6 %all_to_all.85 = f32[32,8,384]{2,1,0:T(8,128)S(1)} all-to-all(f32[32,8,384]{2,1,0:T(8,128)S(1)} %bitcast.347), channel_id=1, replica_groups=mesh['area'=4,'dev'=8] {'area','dev'}, dimensions={0} | all-to-all | bytes 786432 | tf_op jit(solution)/shard_map/all_to_all | solution.py:15
  311.8 1.2 convolution_add_fusion.1
  314.8 31.5 %reduce-scatter.17.cloned.1.call-done = f32[16,144]{1,0:T(8,128)} async-done(((f32[128,144]{1,0:T(8,128)}), f32[16,144]{1,0:T(8,128)}) %reduce-scatter.17.cloned.1.call-update) | async-done | bytes 9232
  350.2 9.2 %all_gather.14 = f32[144,128]{0,1:T(8,128)S(1)} all-gather(f32[144,16]{0,1:T(8,128)S(1)} %pad_maximum_fusion.12), channel_id=1, replica_groups=mesh['area'=4,'dev'=8] {'dev'}, dimensions={1}, use_global_device_ids=true | all-gather | bytes 82944 | tf_op jit(solution)/shard_map/all_gather | solution.py:82
  361.7 4.7 all-to-all-start.5
  367.1 3.2 fusion.9
  370.3 2.3 fusion.8
  372.7 6.9 %all-to-all-done.5 = f32[32,8,384]{2,1,0:T(8,128)} async-done(((f32[32,8,384]{2,1,0:T(8,128)}), f32[32,8,384]{2,1,0:T(8,128)}, u32[]{:S(2)}, u32[]{:S(2)}) %all-to-all-start.5) | async-done | bytes 393248 | tf_op jit(solution)/shard_map/all_to_all | solution.py:19
  379.6 2.0 gather_fusion.8
  381.6 1.5 fusion.2
  383.3 2.4 scatter_fusion.5
  386.5 2.4 scatter_fusion.4
  390.4 1.2 scatter_custom_fusion.9
  391.7 15.6 %all_to_all.86 = f32[32,8,384]{2,1,0:T(8,128)S(1)} all-to-all(f32[32,8,384]{2,1,0:T(8,128)S(1)} %bitcast.342), channel_id=1, replica_groups=mesh['area'=4,'dev'=8] {'area','dev'}, dimensions={0} | all-to-all | bytes 786432 | tf_op jit(solution)/shard_map/all_to_all | solution.py:15
  407.5 1.2 convolution_add_fusion
  410.5 1.2 slice.408
  412.8 1.1 slice.410
  414.0 28.0 %reduce-scatter.19.cloned.1.call-done = f32[16,144]{1,0:T(8,128)} async-done(((f32[128,144]{1,0:T(8,128)}), f32[16,144]{1,0:T(8,128)}) %reduce-scatter.19.cloned.1.call-update) | async-done | bytes 9232
  445.9 9.2 %all_gather.15 = f32[144,128]{0,1:T(8,128)S(1)} all-gather(f32[144,16]{0,1:T(8,128)S(1)} %pad_maximum_fusion.13), channel_id=1, replica_groups=mesh['area'=4,'dev'=8] {'dev'}, dimensions={1}, use_global_device_ids=true | all-gather | bytes 82944 | tf_op jit(solution)/shard_map/all_gather | solution.py:82
  458.1 4.8 all-to-all-start.7
  462.9 4.0 fusion.10
  466.9 3.7 fusion.11
  472.6 3.5 all-to-all-done.7
  477.7 2.4 scatter_fusion.6
  481.1 2.4 scatter_fusion.7
  (317 shorter events, 59.4 us)
Async XLA Ops:
  7.2 6.8 %copy-start = (f32[3,3]{1,0:T(4,128)S(1)}, f32[3,3]{1,0:T(4,128)}, u32[]{:S(2)}) copy-start(f32[3,3]{1,0:T(4,128)} %param.21) | copy-start | bytes 112
  7.2 16.7 %copy-start.67 = (s32[48,2]{0,1:T(2,128)S(1)}, s32[48,2]{0,1:T(2,128)}, u32[]{:S(2)}) copy-start(s32[48,2]{0,1:T(2,128)} %param.25) | copy-start | bytes 1156
  7.2 17.3 %copy-start.55 = (f32[3,3,64]{2,1,0:T(4,128)S(1)}, f32[3,3,64]{2,1,0:T(4,128)}, u32[]{:S(2)}) copy-start(f32[3,3,64]{2,1,0:T(4,128)} %param.24) | copy-start | bytes 6916
  8.1 15.9 %copy-start.68 = (s32[128]{0:T(128)}, s32[128]{0:T(128)S(1)}, u32[]{:S(2)}) copy-start(s32[128]{0:T(128)S(1)} %fusion.178) | copy-start | bytes 1540
  11.5 12.6 %copy-start.29 = (f32[64,3,128]{2,1,0:T(4,128)}, f32[64,3,128]{2,1,0:T(4,128)S(1)}, u32[]{:S(2)}) copy-start(f32[64,3,128]{2,1,0:T(4,128)S(1)} %copy.238) | copy-start | bytes 294916
  13.2 10.9 %copy-start.30 = (f32[64,3,128]{2,1,0:T(4,128)}, f32[64,3,128]{2,1,0:T(4,128)S(1)}, u32[]{:S(2)}) copy-start(f32[64,3,128]{2,1,0:T(4,128)S(1)} %copy.239) | copy-start | bytes 294916
  14.0 10.1 %copy-start.52 = (f32[3,64]{0,1:T(8,128)}, f32[3,64]{0,1:T(8,128)S(1)}, u32[]{:S(2)}) copy-start(f32[3,64]{0,1:T(8,128)S(1)} %copy.92) | copy-start | bytes 2308
  16.4 94.9 %all-to-all-start = ((f32[32,8,384]{2,1,0:T(8,128)}), f32[32,8,384]{2,1,0:T(8,128)}, u32[]{:S(2)}, u32[]{:S(2)}) async-start(f32[32,8,384]{2,1,0:T(8,128)} %bitcast.11), calls=%async_computation | async-start | bytes 786432 | tf_op jit(solution)/shard_map/all_to_all | solution.py:15
  23.8 59.2 %all-reduce.7.cloned.1.call-start = ((), (), s32[]{:S(2)}) async-start(), calls=%async_computation.12 | async-start | bytes 294912 | tf_op jit(solution)/shard_map/psum | solution.py:51
  25.5 4.5 copy-start.39
  25.5 4.6 slice-start
  29.8 82.7 %copy-start.40 = (s32[1,256]{1,0:T(1,128)S(1)}, s32[1,256]{1,0:T(1,128)}, u32[]{:S(2)}) copy-start(s32[1,256]{1,0:T(1,128)} %param.23) | copy-start | bytes 3076
  29.8 84.6 %copy-start.43 = (s32[48]{0:T(128)S(1)}, s32[48]{0:T(128)}, u32[]{:S(2)}) copy-start(s32[48]{0:T(128)} %copy-done.42) | copy-start | bytes 580
  29.8 84.6 %copy-start.46 = (s32[48]{0:T(128)S(1)}, s32[48]{0:T(128)}, u32[]{:S(2)}) copy-start(s32[48]{0:T(128)} %copy-done.45) | copy-start | bytes 580
  29.8 84.6 %copy-start.49 = (s32[64]{0:T(128)S(1)}, s32[64]{0:T(128)}, u32[]{:S(2)}) copy-start(s32[64]{0:T(128)} %copy-done.48) | copy-start | bytes 772
  29.8 120.2 %reduce-scatter.13.cloned.1.call-start = ((), (), s32[]{:S(2)}) async-start(), calls=%async_computation.13 | async-start | bytes 147456
  85.2 83.6 %copy-start.69 = (s32[128]{0:T(128)S(1)}, s32[128]{0:T(128)}, u32[]{:S(2)}) copy-start(s32[128]{0:T(128)} %copy-done.68) | copy-start | bytes 1540
  96.9 71.9 %copy-start.2 = (f32[3,512,128]{2,1,0:T(8,128)S(1)}, f32[3,512,128]{2,1,0:T(8,128)}, u32[]{:S(2)}) copy-start(f32[3,512,128]{2,1,0:T(8,128)} %param.16) | copy-start | bytes 2359300
  97.0 72.1 %copy-start.1 = (f32[3,512,128]{2,1,0:T(8,128)S(1)}, f32[3,512,128]{2,1,0:T(8,128)}, u32[]{:S(2)}) copy-start(f32[3,512,128]{2,1,0:T(8,128)} %param.17) | copy-start | bytes 2359300
  111.2 53.0 %copy-start.28 = (f32[144,144]{1,0:T(8,128)}, f32[144,144]{1,0:T(8,128)S(1)}, u32[]{:S(2)}) copy-start(f32[144,144]{1,0:T(8,128)S(1)} %select_select_fusion) | copy-start | bytes 248836
  135.2 35.4 %copy-start.15 = (f32[2,128,128]{1,2,0:T(8,128)}, f32[2,128,128]{1,2,0:T(8,128)S(1)}, u32[]{:S(2)}) copy-start(f32[2,128,128]{1,2,0:T(8,128)S(1)} %custom-call.25) | copy-start | bytes 393220
  163.0 7.7 %copy-start.19 = (f32[64,128,3]{1,2,0:T(4,128)}, f32[64,128,3]{1,2,0:T(4,128)S(1)}, u32[]{:S(2)}) copy-start(f32[64,128,3]{1,2,0:T(4,128)S(1)} %fusion.44) | copy-start | bytes 294916
  164.2 18.1 %all-to-all-start.1 = ((f32[32,8,384]{2,1,0:T(8,128)}), f32[32,8,384]{2,1,0:T(8,128)S(1)}, u32[]{:S(2)}, u32[]{:S(2)}) async-start(f32[32,8,384]{2,1,0:T(8,128)} %fusion.58), calls=%async_computation.1 | async-start | bytes 786432 | tf_op jit(solution)/shard_map/all_to_all | solution.py:19
  168.8 80.8 %reduce-scatter.15.cloned.1.call-start = ((), (), s32[]{:S(2)}) async-start(), calls=%async_computation.14 | async-start | bytes 147456
  168.9 13.4 %copy-start.66 = (s32[1024]{0:T(1024)}, s32[1024]{0:T(1024)S(1)}, u32[]{:S(2)}) copy-start(s32[1024]{0:T(1024)S(1)} %pad_clamp_fusion) | copy-start | bytes 12292
  172.5 9.7 %copy-start.5 = (f32[3,512]{0,1:T(8,128)}, f32[3,512]{0,1:T(8,128)S(1)}, u32[]{:S(2)}) copy-start(f32[3,512]{0,1:T(8,128)S(1)} %copy.112) | copy-start | bytes 18436
  172.7 98.3 %copy-start.9 = (f32[3,512]{0,1:T(8,128)}, f32[3,512]{0,1:T(8,128)S(1)}, u32[]{:S(2)}) copy-start(f32[3,512]{0,1:T(8,128)S(1)} %copy.109) | copy-start | bytes 18436
  172.7 5.0 %copy-start.14 = (f32[3,511,128]{2,0,1:T(4,128)S(1)}, f32[3,511,128]{2,0,1:T(4,128)}, u32[]{:S(2)}) copy-start(f32[3,511,128]{2,0,1:T(4,128)} %copy.237) | copy-start | bytes 2354692
  182.3 32.1 %copy-start.41 = (s32[1,256]{1,0:T(1,128)S(1)}, s32[1,256]{1,0:T(1,128)}, u32[]{:S(2)}) copy-start(s32[1,256]{1,0:T(1,128)} %param.23) | copy-start | bytes 3076
  183.1 33.1 %copy-start.44 = (s32[48]{0:T(128)S(1)}, s32[48]{0:T(128)}, u32[]{:S(2)}) copy-start(s32[48]{0:T(128)} %copy-done.42) | copy-start | bytes 580
  183.1 33.1 %copy-start.47 = (s32[48]{0:T(128)S(1)}, s32[48]{0:T(128)}, u32[]{:S(2)}) copy-start(s32[48]{0:T(128)} %copy-done.45) | copy-start | bytes 580
  183.2 67.1 %copy-start.16 = (f32[2,128,128]{1,2,0:T(8,128)S(1)}, f32[2,128,128]{1,2,0:T(8,128)}, u32[]{:S(2)}) copy-start(f32[2,128,128]{1,2,0:T(8,128)} %copy-done.15) | copy-start | bytes 393220
  188.2 4.8 copy-start.35
  264.8 6.2 %copy-start.21 = (f32[64,128,3]{1,2,0:T(4,128)}, f32[64,128,3]{1,2,0:T(4,128)S(1)}, u32[]{:S(2)}) copy-start(f32[64,128,3]{1,2,0:T(4,128)S(1)} %fusion.41) | copy-start | bytes 294916
  266.0 17.9 %all-to-all-start.3 = ((f32[32,8,384]{2,1,0:T(8,128)}), f32[32,8,384]{2,1,0:T(8,128)}, u32[]{:S(2)}, u32[]{:S(2)}) async-start(f32[32,8,384]{2,1,0:T(8,128)} %fusion.56), calls=%async_computation.3 | async-start | bytes 786432 | tf_op jit(solution)/shard_map/all_to_all | solution.py:19
  270.7 75.6 %reduce-scatter.17.cloned.1.call-start = ((), (), s32[]{:S(2)}) async-start(), calls=%async_computation.15 | async-start | bytes 147456
  276.8 10.8 %copy-start.61 = (s32[64]{0:T(128)S(1)}, s32[64]{0:T(128)}, u32[]{:S(2)}) copy-start(s32[64]{0:T(128)} %copy-done.60) | copy-start | bytes 772
  276.8 14.0 %copy-start.57 = (s32[64]{0:T(128)S(1)}, s32[64]{0:T(128)}, u32[]{:S(2)}) copy-start(s32[64]{0:T(128)} %copy-done.56) | copy-start | bytes 772
  276.8 17.3 %copy-start.53 = (f32[3,64]{0,1:T(8,128)S(1)}, f32[3,64]{0,1:T(8,128)}, u32[]{:S(2)}) copy-start(f32[3,64]{0,1:T(8,128)} %copy-done.52) | copy-start | bytes 2308
  285.9 27.8 %copy-start.50 = (s32[64]{0:T(128)S(1)}, s32[64]{0:T(128)}, u32[]{:S(2)}) copy-start(s32[64]{0:T(128)} %copy-done.48) | copy-start | bytes 772
  286.0 61.1 %copy-start.17 = (f32[2,128,128]{1,2,0:T(8,128)S(1)}, f32[2,128,128]{1,2,0:T(8,128)}, u32[]{:S(2)}) copy-start(f32[2,128,128]{1,2,0:T(8,128)} %copy-done.15) | copy-start | bytes 393220
  290.8 3.9 copy-start.36
  360.5 6.4 %copy-start.23 = (f32[64,128,3]{1,2,0:T(4,128)}, f32[64,128,3]{1,2,0:T(4,128)S(1)}, u32[]{:S(2)}) copy-start(f32[64,128,3]{1,2,0:T(4,128)S(1)} %fusion.38) | copy-start | bytes 294916
  361.7 17.9 %all-to-all-start.5 = ((f32[32,8,384]{2,1,0:T(8,128)}), f32[32,8,384]{2,1,0:T(8,128)}, u32[]{:S(2)}, u32[]{:S(2)}) async-start(f32[32,8,384]{2,1,0:T(8,128)} %fusion.54), calls=%async_computation.5 | async-start | bytes 786432 | tf_op jit(solution)/shard_map/all_to_all | solution.py:19
  366.4 75.6 %reduce-scatter.19.cloned.1.call-start = ((), (), s32[]{:S(2)}) async-start(), calls=%async_computation.16 | async-start | bytes 147456
  372.7 10.6 %copy-start.62 = (s32[64]{0:T(128)S(1)}, s32[64]{0:T(128)}, u32[]{:S(2)}) copy-start(s32[64]{0:T(128)} %copy-done.60) | copy-start | bytes 772
  372.7 13.8 %copy-start.58 = (s32[64]{0:T(128)S(1)}, s32[64]{0:T(128)}, u32[]{:S(2)}) copy-start(s32[64]{0:T(128)} %copy-done.56) | copy-start | bytes 772
  372.7 17.1 %copy-start.54 = (f32[3,64]{0,1:T(8,128)S(1)}, f32[3,64]{0,1:T(8,128)}, u32[]{:S(2)}) copy-start(f32[3,64]{0,1:T(8,128)} %copy-done.52) | copy-start | bytes 2308
  381.6 27.8 %copy-start.51 = (s32[64]{0:T(128)S(1)}, s32[64]{0:T(128)}, u32[]{:S(2)}) copy-start(s32[64]{0:T(128)} %copy-done.48) | copy-start | bytes 772
  407.3 35.4 %copy-start.18 = (f32[2,128,128]{1,2,0:T(8,128)S(1)}, f32[2,128,128]{1,2,0:T(8,128)}, u32[]{:S(2)}) copy-start(f32[2,128,128]{1,2,0:T(8,128)} %copy-done.15) | copy-start | bytes 393220
  410.5 44.7 %copy-start.27 = (f32[64,3,128]{2,0,1:T(8,128)S(1)}, f32[64,3,128]{2,0,1:T(8,128)}, u32[]{:S(2)}) copy-start(f32[64,3,128]{2,0,1:T(8,128)} %copy-done.26) | copy-start | bytes 294916
  410.5 52.4 %copy-start.4 = (f32[3,512]{0,1:T(8,128)S(1)}, f32[3,512]{0,1:T(8,128)}, u32[]{:S(2)}) copy-start(f32[3,512]{0,1:T(8,128)} %copy-done.3) | copy-start | bytes 18436
  414.0 52.9 %copy-start.8 = (f32[3,512]{0,1:T(8,128)S(1)}, f32[3,512]{0,1:T(8,128)}, u32[]{:S(2)}) copy-start(f32[3,512]{0,1:T(8,128)} %copy-done.5) | copy-start | bytes 18436
  456.9 10.0 %copy-start.25 = (f32[64,128,3]{1,2,0:T(4,128)}, f32[64,128,3]{1,2,0:T(4,128)S(1)}, u32[]{:S(2)}) copy-start(f32[64,128,3]{1,2,0:T(4,128)S(1)} %fusion.35) | copy-start | bytes 294916
  458.1 18.0 %all-to-all-start.7 = ((f32[32,8,384]{2,1,0:T(8,128)}), f32[32,8,384]{2,1,0:T(8,128)S(1)}, u32[]{:S(2)}, u32[]{:S(2)}) async-start(f32[32,8,384]{2,1,0:T(8,128)} %fusion.52), calls=%async_computation.7 | async-start | bytes 786432 | tf_op jit(solution)/shard_map/all_to_all | solution.py:19
  462.9 4.0 copy-start.13
  462.9 7.8 %copy-start.20 = (f32[64,128,3]{1,2,0:T(4,128)S(1)}, f32[64,128,3]{1,2,0:T(4,128)}, u32[]{:S(2)}) copy-start(f32[64,128,3]{1,2,0:T(4,128)} %copy-done.19) | copy-start | bytes 294916
  462.9 7.8 %copy-start.22 = (f32[64,128,3]{1,2,0:T(4,128)S(1)}, f32[64,128,3]{1,2,0:T(4,128)}, u32[]{:S(2)}) copy-start(f32[64,128,3]{1,2,0:T(4,128)} %copy-done.21) | copy-start | bytes 294916
  462.9 7.8 %copy-start.24 = (f32[64,128,3]{1,2,0:T(4,128)S(1)}, f32[64,128,3]{1,2,0:T(4,128)}, u32[]{:S(2)}) copy-start(f32[64,128,3]{1,2,0:T(4,128)} %copy-done.23) | copy-start | bytes 294916
  466.9 10.1 %copy-start.32 = (f32[64,3,128]{2,1,0:T(4,128)S(1)}, f32[64,3,128]{2,1,0:T(4,128)}, u32[]{:S(2)}) copy-start(f32[64,3,128]{2,1,0:T(4,128)} %copy-done.31) | copy-start | bytes 294916
  466.9 10.1 %copy-start.34 = (f32[64,3,128]{2,1,0:T(4,128)S(1)}, f32[64,3,128]{2,1,0:T(4,128)}, u32[]{:S(2)}) copy-start(f32[64,3,128]{2,1,0:T(4,128)} %copy-done.33) | copy-start | bytes 294916
  470.6 7.1 %copy-start.12 = (f32[3,512,128]{2,0,1:T(4,128)S(1)}, f32[3,512,128]{2,0,1:T(4,128)}, u32[]{:S(2)}) copy-start(f32[3,512,128]{2,0,1:T(4,128)} %fusion.10) | copy-start | bytes 2359300
  470.6 7.1 %copy-start.63 = (s32[64]{0:T(128)S(1)}, s32[64]{0:T(128)}, u32[]{:S(2)}) copy-start(s32[64]{0:T(128)} %copy-done.60) | copy-start | bytes 772
  471.8 9.3 %copy-start.59 = (s32[64]{0:T(128)S(1)}, s32[64]{0:T(128)}, u32[]{:S(2)}) copy-start(s32[64]{0:T(128)} %copy-done.56) | copy-start | bytes 772
  (17 other events, 30.7 us)
Sparse Core Ops, SparseCore 0:
  29.9 53.0 all-reduce.6
  115.6 34.3 reduce-scatter.12
  218.2 31.3 reduce-scatter.14
  314.9 31.3 reduce-scatter.16
  410.6 31.3 reduce-scatter.18
where the time goes:
time: 497 us; the launch traced here: 491 us
  waiting for transfers between devices  175 us (35%)
  blocking collectives  87.5 us (18%)
  other arithmetic  76.1 us (15%)
  local copies, waits for them, and re-layouts  69.5 us (14%)
  matrix products  39.5 us (8%)
  starting transfers between devices  26.8 us (5%)
  between operations  17.3 us (3%)
    unnamed x9, waiting for transfers between devices  106 us
    psum x1, waiting for transfers between devices, on_device(): lax.psum(partial_value, 'dev') + jnp.diag(jnp.repeat(link_resist, 3))  51.1 us
    all_to_all x3, blocking collectives, send_ends(): lax.all_to_all(rows, ('area', 'dev'), split_axis=0, concat_axis=0, tiled=...  50.2 us
    all_gather x4, blocking collectives, on_device(): lax.all_gather(solve_links(factor, owned), 'dev', axis=1, tiled=True)  37.3 us
    another operation x7, other arithmetic, on_device(): factor = jnp.linalg.cholesky(matrix)  24.3 us
    another operation x10, other arithmetic, solve_links(): lax.linalg.triangular_solve(factor, lower, left_side=True, lower=True, tr...  20 us
    all_to_all x4, starting transfers between devices, return_volts(): lax.all_to_all(rows, ('area', 'dev'), split_axis=0, concat_axis=0, tiled=...  18.8 us
    all_to_all x4, waiting for transfers between devices, return_volts(): lax.all_to_all(rows, ('area', 'dev'), split_axis=0, concat_axis=0, tiled=...  17.5 us
  transfers between devices with their start and end apart: 10, of which 8 were waited for; matrix products, arithmetic and copies ran while one was open for 19% of the time, Pallas kernels for 0%

commit v1 on v0

--- a/solution.py
+++ b/solution.py
@@ -48,7 +48,9 @@
     partial_value = jnp.einsum(
         "bl,ijb,bm->limj", incidence, bus_impedance, incidence, precision=exact
     ).reshape(3 * link_total, 3 * link_total)
-    matrix = lax.psum(partial_value, "dev") + jnp.diag(jnp.repeat(link_resist, 3))
+    matrix = jnp.sum(lax.all_gather(partial_value, "dev"), axis=0) + jnp.diag(
+        jnp.repeat(link_resist, 3)
+    )
     factor = jnp.linalg.cholesky(matrix)
     place_overall_sum = recv_bus.shape[1]
     one_hot = (jnp.arange(bus_total, dtype=jnp.int32)[:, None] == recv_bus).astype(jnp.float32)

time: 497 us -> 476 us (0.958)
  waiting for transfers between devices: 175 us -> 142 us
  blocking collectives: 87.5 us -> 101 us
    psum x1 -> x0, waiting for transfers between devices: 51.1 us -> none  [on_device(): lax.psum(partial_value, 'dev') + jnp.diag(jnp.repeat(link_resist, 3))]
    unnamed x9 -> x8, waiting for transfers between devices: 106 us -> 124 us
    all_gather x0 -> x1, blocking collectives: none -> 13.2 us  [on_device(): lax.all_gather(partial_value, 'dev')]
    unnamed x159 -> x157, local copies, waits for them, and re-layouts: 12.9 us -> 12.8 us
  transfers between devices with their start and end apart: 10 -> 9, of which waited for: 8 -> 7; matrix products, arithmetic and copies ran while one was open for 19% -> 19% of each run, Pallas kernels for 0% -> 0%
where the time goes in v1:
time: 476 us; the launch traced here: 470 us
  waiting for transfers between devices  142 us (30%)
  blocking collectives  101 us (21%)
  other arithmetic  74.9 us (16%)
  local copies, waits for them, and re-layouts  69.6 us (15%)
  matrix products  39.2 us (8%)
  starting transfers between devices  26.6 us (6%)
  between operations  17.2 us (4%)
    unnamed x8, waiting for transfers between devices  124 us
    all_to_all x3, blocking collectives, send_ends(): lax.all_to_all(rows, ('area', 'dev'), split_axis=0, concat_axis=0, tiled=...  50.2 us
    all_gather x4, blocking collectives, on_device(): lax.all_gather(solve_links(factor, owned), 'dev', axis=1, tiled=True)  37.3 us
    another operation x7, other arithmetic, on_device(): factor = jnp.linalg.cholesky(matrix)  24.4 us
    another operation x10, other arithmetic, solve_links(): lax.linalg.triangular_solve(factor, lower, left_side=True, lower=True, tr...  20 us
    all_to_all x4, starting transfers between devices, return_volts(): lax.all_to_all(rows, ('area', 'dev'), split_axis=0, concat_axis=0, tiled=...  18.8 us
    all_to_all x4, waiting for transfers between devices, return_volts(): lax.all_to_all(rows, ('area', 'dev'), split_axis=0, concat_axis=0, tiled=...  17.4 us
    add x4, other arithmetic, on_device(): (1.0 - seg_reflect)[:, :, None] * jnp.roll(forward, 1, axis=1)  15.5 us
  transfers between devices with their start and end apart: 9, of which 7 were waited for; matrix products, arithmetic and copies ran while one was open for 19% of the time, Pallas kernels for 0%

profile of v1, /device:TPU:0, one launch (start us, length us, event | category | flops | bytes accessed | tf_op | source)
XLA Modules:
  0.0 469.9 jit_solution(14852886155102805950)
XLA Ops:
  9.7 1.6 gather_fusion.1
  11.5 1.6 gather_fusion
  14.7 1.7 scatter_custom_fusion
  16.4 7.4 %all-to-all-start = ((f32[32,8,384]{2,1,0:T(8,128)}), f32[32,8,384]{2,1,0:T(8,128)}, u32[]{:S(2)}, u32[]{:S(2)}) async-start(f32[32,8,384]{2,1,0:T(8,128)} %bitcast.11), calls=%async_computation | async-start | bytes 786432 | tf_op jit(solution)/shard_map/all_to_all | solution.py:15
  26.3 2.1 copy.98
  28.4 2.1 all_gather_reshape.3
  30.5 13.2 %all_gather.15 = f32[8,144,144]{2,1,0:T(8,128)S(1)} all-gather(f32[1,144,144]{2,1,0:T(8,128)} %all_gather_reshape.3), channel_id=1, replica_groups=mesh['area'=4,'dev'=8] {'dev'}, dimensions={0}, use_global_device_ids=true | all-gather | bytes 746496 | tf_op jit(solution)/shard_map/all_gather | solution.py:51
  44.9 11.7 %cholesky.50 = f32[128,128]{1,0:T(8,128)S(1)} custom-call(f32[128,128]{1,0:T(8,128)S(1)} %cholesky.121), custom_call_target="Cholesky" | custom-call | tf_op jit(solution)/shard_map/jit(cholesky)/cholesky | solution.py:54
  56.7 9.8 %custom-call.17 = f32[1,128,128]{1,2,0:T(8,128)S(1)} custom-call(f32[1,128,128]{2,1,0:T(8,128)S(1)} %get-tuple-element.103), custom_call_target="InvertDiagBlocksLowerTriangular" | custom-call | tf_op jit(solution)/shard_map/jit(cholesky)/cholesky | solution.py:54
  66.9 1.5 cholesky.108
  71.2 19.7 %custom-call.25 = f32[2,128,128]{1,2,0:T(8,128)S(1)} custom-call(f32[2,128,128]{2,1,0:T(8,128)S(1)} %pad_maximum_fusion.9), custom_call_target="InvertDiagBlocksLowerTriangular" | custom-call | tf_op jit(solution)/shard_map/triangular_solve/custom-call.4 | solution.py:11
  90.9 1.2 copy.97
  92.1 1.2 convolution_add_fusion.3
  95.2 33.1 %reduce-scatter.13.cloned.1.call-done = f32[16,144]{1,0:T(8,128)} async-done(((f32[128,144]{1,0:T(8,128)}), f32[16,144]{1,0:T(8,128)}) %reduce-scatter.13.cloned.1.call-update) | async-done | bytes 9232
  130.9 9.4 %all_gather.16 = f32[144,128]{0,1:T(8,128)S(1)} all-gather(f32[144,16]{0,1:T(8,128)S(1)} %pad_maximum_fusion.10), channel_id=1, replica_groups=mesh['area'=4,'dev'=8] {'dev'}, dimensions={1}, use_global_device_ids=true | all-gather | bytes 82944 | tf_op jit(solution)/shard_map/all_gather | solution.py:84
  142.5 4.6 all-to-all-start.1
  148.0 1.5 copy.233
  149.8 1.5 copy.236
  151.6 5.0 %fusion.5 = f32[3,512,128]{2,0,1:T(4,128)S(1)} fusion(f32[3,511,128]{2,0,1:T(4,128)} %copy.233, f32[3,1,128]{2,0,1:T(4,128)S(1)} %copy.234, f32[3,512]{0,1:T(8,128)S(1)} %copy.116, f32[3,512]{0,1:T(8,128)S(1)} %copy.113, f32[3,512,128]{2,1,0:T(8,128)S(1)} %copy-done.2), kind=kLoop, calls=%fused_computation.61 | loop fusion | flops 786432 | bytes 2371584 | tf_op jit(solution)/shard_map/add | solution.py:100
  156.6 4.5 fusion.4
  162.2 1.6 fusion
  163.8 2.6 scatter_fusion.1
  167.2 2.6 scatter_fusion
  170.5 1.4 convolution_multiply_fusion.2
  172.0 1.2 scatter_custom_fusion.3
  173.3 18.9 %all_to_all.84 = f32[32,8,384]{2,1,0:T(8,128)} all-to-all(f32[32,8,384]{2,1,0:T(8,128)S(1)} %bitcast.341), channel_id=1, replica_groups=mesh['area'=4,'dev'=8] {'area','dev'}, dimensions={0} | all-to-all | bytes 786432 | tf_op jit(solution)/shard_map/all_to_all | solution.py:15
  192.2 1.2 copy.119
  193.4 1.2 convolution_add_fusion.2
  196.9 31.6 %reduce-scatter.15.cloned.1.call-done = f32[16,144]{1,0:T(8,128)} async-done(((f32[128,144]{1,0:T(8,128)}), f32[16,144]{1,0:T(8,128)}) %reduce-scatter.15.cloned.1.call-update) | async-done | bytes 9232
  232.4 9.6 %all_gather.17 = f32[144,128]{0,1:T(8,128)S(1)} all-gather(f32[144,16]{0,1:T(8,128)S(1)} %pad_maximum_fusion.11), channel_id=1, replica_groups=mesh['area'=4,'dev'=8] {'dev'}, dimensions={1}, use_global_device_ids=true | all-gather | bytes 82944 | tf_op jit(solution)/shard_map/all_gather | solution.py:84
  244.8 4.7 %all-to-all-start.3 = ((f32[32,8,384]{2,1,0:T(8,128)}), f32[32,8,384]{2,1,0:T(8,128)}, u32[]{:S(2)}, u32[]{:S(2)}) async-start(f32[32,8,384]{2,1,0:T(8,128)} %fusion.55), calls=%async_computation.3 | async-start | bytes 786432 | tf_op jit(solution)/shard_map/all_to_all | solution.py:19
  250.0 3.2 fusion.7
  253.3 2.3 fusion.6
  255.6 7.1 %all-to-all-done.3 = f32[32,8,384]{2,1,0:T(8,128)} async-done(((f32[32,8,384]{2,1,0:T(8,128)}), f32[32,8,384]{2,1,0:T(8,128)}, u32[]{:S(2)}, u32[]{:S(2)}) %all-to-all-start.3) | async-done | bytes 393248 | tf_op jit(solution)/shard_map/all_to_all | solution.py:19
  262.7 2.0 gather_fusion.5
  264.8 1.6 fusion.1
  266.4 2.4 scatter_fusion.3
  269.7 2.4 scatter_fusion.2
  273.6 1.2 scatter_custom_fusion.6
  274.9 15.6 %all_to_all.85 = f32[32,8,384]{2,1,0:T(8,128)S(1)} all-to-all(f32[32,8,384]{2,1,0:T(8,128)S(1)} %bitcast.344), channel_id=1, replica_groups=mesh['area'=4,'dev'=8] {'area','dev'}, dimensions={0} | all-to-all | bytes 786432 | tf_op jit(solution)/shard_map/all_to_all | solution.py:15
  290.7 1.2 convolution_add_fusion.1
  293.6 31.5 %reduce-scatter.17.cloned.1.call-done = f32[16,144]{1,0:T(8,128)} async-done(((f32[128,144]{1,0:T(8,128)}), f32[16,144]{1,0:T(8,128)}) %reduce-scatter.17.cloned.1.call-update) | async-done | bytes 9232
  329.1 9.2 %all_gather.18 = f32[144,128]{0,1:T(8,128)S(1)} all-gather(f32[144,16]{0,1:T(8,128)S(1)} %pad_maximum_fusion.12), channel_id=1, replica_groups=mesh['area'=4,'dev'=8] {'dev'}, dimensions={1}, use_global_device_ids=true | all-gather | bytes 82944 | tf_op jit(solution)/shard_map/all_gather | solution.py:84
  340.5 4.7 %all-to-all-start.5 = ((f32[32,8,384]{2,1,0:T(8,128)}), f32[32,8,384]{2,1,0:T(8,128)}, u32[]{:S(2)}, u32[]{:S(2)}) async-start(f32[32,8,384]{2,1,0:T(8,128)} %fusion.53), calls=%async_computation.5 | async-start | bytes 786432 | tf_op jit(solution)/shard_map/all_to_all | solution.py:19
  345.9 3.2 fusion.9
  349.2 2.3 fusion.8
  351.5 6.9 %all-to-all-done.5 = f32[32,8,384]{2,1,0:T(8,128)} async-done(((f32[32,8,384]{2,1,0:T(8,128)}), f32[32,8,384]{2,1,0:T(8,128)}, u32[]{:S(2)}, u32[]{:S(2)}) %all-to-all-start.5) | async-done | bytes 393248 | tf_op jit(solution)/shard_map/all_to_all | solution.py:19
  358.4 2.0 gather_fusion.8
  360.5 1.5 fusion.2
  362.1 2.4 scatter_fusion.5
  365.3 2.4 scatter_fusion.4
  369.3 1.2 scatter_custom_fusion.9
  370.5 15.6 %all_to_all.86 = f32[32,8,384]{2,1,0:T(8,128)S(1)} all-to-all(f32[32,8,384]{2,1,0:T(8,128)S(1)} %bitcast.339), channel_id=1, replica_groups=mesh['area'=4,'dev'=8] {'area','dev'}, dimensions={0} | all-to-all | bytes 786432 | tf_op jit(solution)/shard_map/all_to_all | solution.py:15
  386.3 1.2 convolution_add_fusion
  389.3 1.2 slice.408
  391.6 1.2 slice.410
  392.8 28.1 %reduce-scatter.19.cloned.1.call-done = f32[16,144]{1,0:T(8,128)} async-done(((f32[128,144]{1,0:T(8,128)}), f32[16,144]{1,0:T(8,128)}) %reduce-scatter.19.cloned.1.call-update) | async-done | bytes 9232
  424.7 9.2 %all_gather.19 = f32[144,128]{0,1:T(8,128)S(1)} all-gather(f32[144,16]{0,1:T(8,128)S(1)} %pad_maximum_fusion.13), channel_id=1, replica_groups=mesh['area'=4,'dev'=8] {'dev'}, dimensions={1}, use_global_device_ids=true | all-gather | bytes 82944 | tf_op jit(solution)/shard_map/all_gather | solution.py:84
  436.8 4.8 %all-to-all-start.7 = ((f32[32,8,384]{2,1,0:T(8,128)}), f32[32,8,384]{2,1,0:T(8,128)S(1)}, u32[]{:S(2)}, u32[]{:S(2)}) async-start(f32[32,8,384]{2,1,0:T(8,128)} %fusion.51), calls=%async_computation.7 | async-start | bytes 786432 | tf_op jit(solution)/shard_map/all_to_all | solution.py:19
  441.7 4.0 fusion.10
  445.7 3.7 fusion.11
  451.3 3.5 all-to-all-done.7
  456.4 2.4 scatter_fusion.6
  459.8 2.4 scatter_fusion.7
  (313 shorter events, 57.8 us)
Async XLA Ops:
  7.2 6.8 %copy-start = (f32[3,3]{1,0:T(4,128)S(1)}, f32[3,3]{1,0:T(4,128)}, u32[]{:S(2)}) copy-start(f32[3,3]{1,0:T(4,128)} %param.21) | copy-start | bytes 112
  7.2 16.7 %copy-start.55 = (f32[3,3,64]{2,1,0:T(4,128)S(1)}, f32[3,3,64]{2,1,0:T(4,128)}, u32[]{:S(2)}) copy-start(f32[3,3,64]{2,1,0:T(4,128)} %param.24) | copy-start | bytes 6916
  7.2 17.5 %copy-start.66 = (s32[48,2]{0,1:T(2,128)S(1)}, s32[48,2]{0,1:T(2,128)}, u32[]{:S(2)}) copy-start(s32[48,2]{0,1:T(2,128)} %param.25) | copy-start | bytes 1156
  8.1 16.7 %copy-start.67 = (s32[128]{0:T(128)}, s32[128]{0:T(128)S(1)}, u32[]{:S(2)}) copy-start(s32[128]{0:T(128)S(1)} %fusion.177) | copy-start | bytes 1540
  11.5 13.4 %copy-start.30 = (f32[64,3,128]{2,1,0:T(4,128)}, f32[64,3,128]{2,1,0:T(4,128)S(1)}, u32[]{:S(2)}) copy-start(f32[64,3,128]{2,1,0:T(4,128)S(1)} %copy.237) | copy-start | bytes 294916
  13.2 11.6 %copy-start.31 = (f32[64,3,128]{2,1,0:T(4,128)}, f32[64,3,128]{2,1,0:T(4,128)S(1)}, u32[]{:S(2)}) copy-start(f32[64,3,128]{2,1,0:T(4,128)S(1)} %copy.238) | copy-start | bytes 294916
  14.0 10.8 %copy-start.52 = (f32[3,64]{0,1:T(8,128)}, f32[3,64]{0,1:T(8,128)S(1)}, u32[]{:S(2)}) copy-start(f32[3,64]{0,1:T(8,128)S(1)} %copy.91) | copy-start | bytes 2308
  16.4 74.5 %all-to-all-start = ((f32[32,8,384]{2,1,0:T(8,128)}), f32[32,8,384]{2,1,0:T(8,128)}, u32[]{:S(2)}, u32[]{:S(2)}) async-start(f32[32,8,384]{2,1,0:T(8,128)} %bitcast.11), calls=%async_computation | async-start | bytes 786432 | tf_op jit(solution)/shard_map/all_to_all | solution.py:15
  23.9 104.5 %reduce-scatter.13.cloned.1.call-start = ((), (), s32[]{:S(2)}) async-start(), calls=%async_computation.12 | async-start | bytes 147456
  28.4 28.3 %copy-start.40 = (f32[3,512]{1,0:T(4,128)S(1)}, f32[3,512]{1,0:T(4,128)}, u32[]{:S(2)}) copy-start(f32[3,512]{1,0:T(4,128)} %param.18) | copy-start | bytes 18436
  30.5 61.6 %copy-start.41 = (s32[1,256]{1,0:T(1,128)S(1)}, s32[1,256]{1,0:T(1,128)}, u32[]{:S(2)}) copy-start(s32[1,256]{1,0:T(1,128)} %param.23) | copy-start | bytes 3076
  30.5 62.8 %copy-start.1 = (f32[3,3,64]{1,0,2:T(4,128)S(1)}, f32[3,3,64]{1,0,2:T(4,128)}, u32[]{:S(2)}) copy-start(f32[3,3,64]{1,0,2:T(4,128)} %copy.101) | copy-start | bytes 6916
  30.5 63.4 %copy-start.43 = (s32[48]{0:T(128)S(1)}, s32[48]{0:T(128)}, u32[]{:S(2)}) copy-start(s32[48]{0:T(128)} %copy-done.42) | copy-start | bytes 580
  30.5 63.5 %copy-start.46 = (s32[48]{0:T(128)S(1)}, s32[48]{0:T(128)}, u32[]{:S(2)}) copy-start(s32[48]{0:T(128)} %copy-done.45) | copy-start | bytes 580
  30.5 63.5 %copy-start.49 = (s32[64]{0:T(128)S(1)}, s32[64]{0:T(128)}, u32[]{:S(2)}) copy-start(s32[64]{0:T(128)} %copy-done.48) | copy-start | bytes 772
  30.5 64.6 %slice-start = ((f32[3,512]{1,0:T(4,128)}), f32[3,1]{1,0:T(4,128)S(1)}, s32[]{:S(2)}) async-start(f32[3,512]{1,0:T(4,128)} %param.18), calls=%async_computation.16 | async-start | bytes 4096 | tf_op jit(solution)/shard_map/jit(_roll_static)/slice | solution.py:58
  56.6 90.6 %copy-start.68 = (s32[128]{0:T(128)S(1)}, s32[128]{0:T(128)}, u32[]{:S(2)}) copy-start(s32[128]{0:T(128)} %copy-done.67) | copy-start | bytes 1540
  56.6 91.2 %copy-start.3 = (f32[3,512,128]{2,1,0:T(8,128)S(1)}, f32[3,512,128]{2,1,0:T(8,128)}, u32[]{:S(2)}) copy-start(f32[3,512,128]{2,1,0:T(8,128)} %param.16) | copy-start | bytes 2359300
  66.7 81.2 %copy-start.2 = (f32[3,512,128]{2,1,0:T(8,128)S(1)}, f32[3,512,128]{2,1,0:T(8,128)}, u32[]{:S(2)}) copy-start(f32[3,512,128]{2,1,0:T(8,128)} %param.17) | copy-start | bytes 2359300
  71.0 76.9 %copy-start.29 = (f32[144,144]{1,0:T(8,128)}, f32[144,144]{1,0:T(8,128)S(1)}, u32[]{:S(2)}) copy-start(f32[144,144]{1,0:T(8,128)S(1)} %select_select_fusion) | copy-start | bytes 248836
  90.9 57.2 %copy-start.16 = (f32[2,128,128]{1,2,0:T(8,128)}, f32[2,128,128]{1,2,0:T(8,128)S(1)}, u32[]{:S(2)}) copy-start(f32[2,128,128]{1,2,0:T(8,128)S(1)} %custom-call.25) | copy-start | bytes 393220
  141.4 8.2 %copy-start.20 = (f32[64,128,3]{1,2,0:T(4,128)}, f32[64,128,3]{1,2,0:T(4,128)S(1)}, u32[]{:S(2)}) copy-start(f32[64,128,3]{1,2,0:T(4,128)S(1)} %fusion.43) | copy-start | bytes 294916
  142.5 18.6 %all-to-all-start.1 = ((f32[32,8,384]{2,1,0:T(8,128)}), f32[32,8,384]{2,1,0:T(8,128)S(1)}, u32[]{:S(2)}, u32[]{:S(2)}) async-start(f32[32,8,384]{2,1,0:T(8,128)} %fusion.57), calls=%async_computation.1 | async-start | bytes 786432 | tf_op jit(solution)/shard_map/all_to_all | solution.py:19
  147.1 81.4 %reduce-scatter.15.cloned.1.call-start = ((), (), s32[]{:S(2)}) async-start(), calls=%async_computation.13 | async-start | bytes 147456
  151.4 9.7 %copy-start.6 = (f32[3,512]{0,1:T(8,128)}, f32[3,512]{0,1:T(8,128)S(1)}, u32[]{:S(2)}) copy-start(f32[3,512]{0,1:T(8,128)S(1)} %copy.111) | copy-start | bytes 18436
  151.6 98.2 %copy-start.10 = (f32[3,512]{0,1:T(8,128)}, f32[3,512]{0,1:T(8,128)S(1)}, u32[]{:S(2)}) copy-start(f32[3,512]{0,1:T(8,128)S(1)} %copy.108) | copy-start | bytes 18436
  151.6 5.0 %copy-start.15 = (f32[3,511,128]{2,0,1:T(4,128)S(1)}, f32[3,511,128]{2,0,1:T(4,128)}, u32[]{:S(2)}) copy-start(f32[3,511,128]{2,0,1:T(4,128)} %copy.236) | copy-start | bytes 2354692
  162.1 33.1 %copy-start.44 = (s32[48]{0:T(128)S(1)}, s32[48]{0:T(128)}, u32[]{:S(2)}) copy-start(s32[48]{0:T(128)} %copy-done.42) | copy-start | bytes 580
  162.1 33.1 %copy-start.47 = (s32[48]{0:T(128)S(1)}, s32[48]{0:T(128)}, u32[]{:S(2)}) copy-start(s32[48]{0:T(128)} %copy-done.45) | copy-start | bytes 580
  162.2 67.0 %copy-start.17 = (f32[2,128,128]{1,2,0:T(8,128)S(1)}, f32[2,128,128]{1,2,0:T(8,128)}, u32[]{:S(2)}) copy-start(f32[2,128,128]{1,2,0:T(8,128)} %copy-done.16) | copy-start | bytes 393220
  167.2 4.8 %copy-start.36 = (f32[64,3,128]{2,1,0:T(4,128)}, f32[64,3,128]{2,1,0:T(4,128)S(1)}, u32[]{:S(2)}) copy-start(f32[64,3,128]{2,1,0:T(4,128)S(1)} %gather_fusion.4) | copy-start | bytes 294916
  243.7 6.2 %copy-start.22 = (f32[64,128,3]{1,2,0:T(4,128)}, f32[64,128,3]{1,2,0:T(4,128)S(1)}, u32[]{:S(2)}) copy-start(f32[64,128,3]{1,2,0:T(4,128)S(1)} %fusion.40) | copy-start | bytes 294916
  244.8 17.9 %all-to-all-start.3 = ((f32[32,8,384]{2,1,0:T(8,128)}), f32[32,8,384]{2,1,0:T(8,128)}, u32[]{:S(2)}, u32[]{:S(2)}) async-start(f32[32,8,384]{2,1,0:T(8,128)} %fusion.55), calls=%async_computation.3 | async-start | bytes 786432 | tf_op jit(solution)/shard_map/all_to_all | solution.py:19
  249.5 75.6 %reduce-scatter.17.cloned.1.call-start = ((), (), s32[]{:S(2)}) async-start(), calls=%async_computation.14 | async-start | bytes 147456
  249.6 3.7 copy-start.7
  255.6 10.8 %copy-start.61 = (s32[64]{0:T(128)S(1)}, s32[64]{0:T(128)}, u32[]{:S(2)}) copy-start(s32[64]{0:T(128)} %copy-done.60) | copy-start | bytes 772
  255.6 14.0 %copy-start.57 = (s32[64]{0:T(128)S(1)}, s32[64]{0:T(128)}, u32[]{:S(2)}) copy-start(s32[64]{0:T(128)} %copy-done.56) | copy-start | bytes 772
  255.6 17.3 %copy-start.53 = (f32[3,64]{0,1:T(8,128)S(1)}, f32[3,64]{0,1:T(8,128)}, u32[]{:S(2)}) copy-start(f32[3,64]{0,1:T(8,128)} %copy-done.52) | copy-start | bytes 2308
  264.7 27.8 %copy-start.50 = (s32[64]{0:T(128)S(1)}, s32[64]{0:T(128)}, u32[]{:S(2)}) copy-start(s32[64]{0:T(128)} %copy-done.48) | copy-start | bytes 772
  264.8 61.1 %copy-start.18 = (f32[2,128,128]{1,2,0:T(8,128)S(1)}, f32[2,128,128]{1,2,0:T(8,128)}, u32[]{:S(2)}) copy-start(f32[2,128,128]{1,2,0:T(8,128)} %copy-done.16) | copy-start | bytes 393220
  269.7 3.9 copy-start.37
  339.3 6.4 %copy-start.24 = (f32[64,128,3]{1,2,0:T(4,128)}, f32[64,128,3]{1,2,0:T(4,128)S(1)}, u32[]{:S(2)}) copy-start(f32[64,128,3]{1,2,0:T(4,128)S(1)} %fusion.37) | copy-start | bytes 294916
  340.5 17.9 %all-to-all-start.5 = ((f32[32,8,384]{2,1,0:T(8,128)}), f32[32,8,384]{2,1,0:T(8,128)}, u32[]{:S(2)}, u32[]{:S(2)}) async-start(f32[32,8,384]{2,1,0:T(8,128)} %fusion.53), calls=%async_computation.5 | async-start | bytes 786432 | tf_op jit(solution)/shard_map/all_to_all | solution.py:19
  345.2 75.6 %reduce-scatter.19.cloned.1.call-start = ((), (), s32[]{:S(2)}) async-start(), calls=%async_computation.15 | async-start | bytes 147456
  351.5 10.6 %copy-start.62 = (s32[64]{0:T(128)S(1)}, s32[64]{0:T(128)}, u32[]{:S(2)}) copy-start(s32[64]{0:T(128)} %copy-done.60) | copy-start | bytes 772
  351.5 13.8 %copy-start.58 = (s32[64]{0:T(128)S(1)}, s32[64]{0:T(128)}, u32[]{:S(2)}) copy-start(s32[64]{0:T(128)} %copy-done.56) | copy-start | bytes 772
  351.5 17.1 %copy-start.54 = (f32[3,64]{0,1:T(8,128)S(1)}, f32[3,64]{0,1:T(8,128)}, u32[]{:S(2)}) copy-start(f32[3,64]{0,1:T(8,128)} %copy-done.52) | copy-start | bytes 2308
  360.4 27.8 %copy-start.51 = (s32[64]{0:T(128)S(1)}, s32[64]{0:T(128)}, u32[]{:S(2)}) copy-start(s32[64]{0:T(128)} %copy-done.48) | copy-start | bytes 772
  365.3 3.9 copy-start.32
  386.1 35.4 %copy-start.19 = (f32[2,128,128]{1,2,0:T(8,128)S(1)}, f32[2,128,128]{1,2,0:T(8,128)}, u32[]{:S(2)}) copy-start(f32[2,128,128]{1,2,0:T(8,128)} %copy-done.16) | copy-start | bytes 393220
  389.3 44.7 %copy-start.28 = (f32[64,3,128]{2,0,1:T(8,128)S(1)}, f32[64,3,128]{2,0,1:T(8,128)}, u32[]{:S(2)}) copy-start(f32[64,3,128]{2,0,1:T(8,128)} %copy-done.27) | copy-start | bytes 294916
  389.3 52.3 %copy-start.5 = (f32[3,512]{0,1:T(8,128)S(1)}, f32[3,512]{0,1:T(8,128)}, u32[]{:S(2)}) copy-start(f32[3,512]{0,1:T(8,128)} %copy-done.4) | copy-start | bytes 18436
  392.8 52.9 %copy-start.9 = (f32[3,512]{0,1:T(8,128)S(1)}, f32[3,512]{0,1:T(8,128)}, u32[]{:S(2)}) copy-start(f32[3,512]{0,1:T(8,128)} %copy-done.6) | copy-start | bytes 18436
  435.6 10.0 %copy-start.26 = (f32[64,128,3]{1,2,0:T(4,128)}, f32[64,128,3]{1,2,0:T(4,128)S(1)}, u32[]{:S(2)}) copy-start(f32[64,128,3]{1,2,0:T(4,128)S(1)} %fusion.34) | copy-start | bytes 294916
  436.8 18.0 %all-to-all-start.7 = ((f32[32,8,384]{2,1,0:T(8,128)}), f32[32,8,384]{2,1,0:T(8,128)S(1)}, u32[]{:S(2)}, u32[]{:S(2)}) async-start(f32[32,8,384]{2,1,0:T(8,128)} %fusion.51), calls=%async_computation.7 | async-start | bytes 786432 | tf_op jit(solution)/shard_map/all_to_all | solution.py:19
  441.6 4.0 copy-start.14
  441.6 7.8 %copy-start.21 = (f32[64,128,3]{1,2,0:T(4,128)S(1)}, f32[64,128,3]{1,2,0:T(4,128)}, u32[]{:S(2)}) copy-start(f32[64,128,3]{1,2,0:T(4,128)} %copy-done.20) | copy-start | bytes 294916
  441.6 7.8 %copy-start.23 = (f32[64,128,3]{1,2,0:T(4,128)S(1)}, f32[64,128,3]{1,2,0:T(4,128)}, u32[]{:S(2)}) copy-start(f32[64,128,3]{1,2,0:T(4,128)} %copy-done.22) | copy-start | bytes 294916
  441.7 7.8 %copy-start.25 = (f32[64,128,3]{1,2,0:T(4,128)S(1)}, f32[64,128,3]{1,2,0:T(4,128)}, u32[]{:S(2)}) copy-start(f32[64,128,3]{1,2,0:T(4,128)} %copy-done.24) | copy-start | bytes 294916
  445.7 10.1 %copy-start.33 = (f32[64,3,128]{2,1,0:T(4,128)S(1)}, f32[64,3,128]{2,1,0:T(4,128)}, u32[]{:S(2)}) copy-start(f32[64,3,128]{2,1,0:T(4,128)} %copy-done.32) | copy-start | bytes 294916
  445.7 10.1 %copy-start.35 = (f32[64,3,128]{2,1,0:T(4,128)S(1)}, f32[64,3,128]{2,1,0:T(4,128)}, u32[]{:S(2)}) copy-start(f32[64,3,128]{2,1,0:T(4,128)} %copy-done.34) | copy-start | bytes 294916
  449.4 7.0 %copy-start.13 = (f32[3,512,128]{2,0,1:T(4,128)S(1)}, f32[3,512,128]{2,0,1:T(4,128)}, u32[]{:S(2)}) copy-start(f32[3,512,128]{2,0,1:T(4,128)} %fusion.10) | copy-start | bytes 2359300
  449.4 7.0 %copy-start.63 = (s32[64]{0:T(128)S(1)}, s32[64]{0:T(128)}, u32[]{:S(2)}) copy-start(s32[64]{0:T(128)} %copy-done.60) | copy-start | bytes 772
  450.5 9.3 %copy-start.59 = (s32[64]{0:T(128)S(1)}, s32[64]{0:T(128)}, u32[]{:S(2)}) copy-start(s32[64]{0:T(128)} %copy-done.56) | copy-start | bytes 772
  (15 other events, 23.0 us)
Sparse Core Ops, SparseCore 0:
  95.3 33.0 reduce-scatter.12
  197.1 31.3 reduce-scatter.14
  293.8 31.3 reduce-scatter.16
  389.4 31.3 reduce-scatter.18
